TPU v7x, 32 devices: a whole 2x2x4 slice. The times are simulated.
32 devices in a mesh: groups: 2 (over y), expert: 4 (over x, core), tensor: 4 (over z).
Axes of the slice: x: 2, y: 2, z: 4, core: 2. Of those that a mesh axis runs over, the one named last changes fastest.
Arguments:
- tokens: bfloat16 [1024, 3072], P(('groups', 'expert'), 'tensor'), parts along dimension 0, may hold values from -6 to 6
- teacher_routes: int32 [1024, 2], P(('groups', 'expert')), parts along dimension 0, may hold values from 0 to 3, all different within a row; in each aligned block of 128 rows (0 to 127, 128 to 255, ...) at most 80 rows name the same one
- teacher_share: float32 [1024], P(('groups', 'expert')), parts along dimension 0, may hold values from 0.1 to 0.9
- student_routes: int32 [1024, 1], P(('groups', 'expert')), parts along dimension 0, may hold values from 0 to 3; in each aligned block of 128 rows (0 to 127, 128 to 255, ...) at most 48 rows name the same one
- gate_weight: bfloat16 [4, 3072, 8192], P('expert', None, 'tensor'), may hold values from -0.109375 to 0.109375
- up_weight: bfloat16 [4, 3072, 8192], P('expert', None, 'tensor'), may hold values from -0.109375 to 0.109375
- down_weight: bfloat16 [4, 8192, 3072], P('expert', 'tensor'), may hold values from -0.0625 to 0.0625
- enc_weight: float32 [4, 3072, 4096], P('expert', 'tensor'), may hold values from -0.109375 to 0.109375
- enc_bias: float32 [4, 4096], P('expert'), may hold values from -3 to 3
- dec_weight: float32 [4, 4096, 3072], P('expert', None, 'tensor'), may hold values from -0.09375 to 0.09375
Outputs:
- enc_grad: float32 [8, 3072, 4096], P(('groups', 'expert'), 'tensor'), parts along dimension 0
- bias_grad: float32 [8, 4096], P(('groups', 'expert')), parts along dimension 0
- dec_grad: float32 [8, 4096, 3072], P(('groups', 'expert'), None, 'tensor'), parts along dimension 0
There are 2 independent parts, one for each index of `groups`. A program takes and returns all parts, laid end to end along the dimension named above; an argument that names none is the same for every part. Nothing has to cross between parts.
Inputs may be any that keep to these rules, and one draw needn't show every extreme that they name: `teacher_routes`: each row names two different experts. In each aligned block of 128 rows (the tokens of one index of expert) no expert is named more than 80 times, and in some blocks one is named exactly 80 times. `student_routes`: in each aligned block of 128 rows no dictionary is named more than 48 times, and in some blocks one is named exactly 48 times.
All inputs are finite; a program needn't handle non-finite values.
Results may differ from a plain program's by a relative error of at most 0.005.
Values may be sent and summed in bfloat16 or wider, within the bound.
A program may use at most 192 MiB of HBM per device.

v0:
```python
import jax
import jax.numpy as jnp
from jax import lax
from jax.sharding import PartitionSpec as P

EXPERTS = 4
DICTS = 4
CAP = 80
CAP_S = 48


error_scale = 0.0625


def activation(values):
    return jax.nn.gelu(values, approximate=True)


def slot_table(routes, group_count, capacity):
    length, pick_count = routes.shape
    flat_ids = routes.reshape(length * pick_count)
    onehot = (flat_ids[:, None] == jnp.arange(group_count, dtype=jnp.int32)[None, :]).astype(
        jnp.int32
    )
    before = jnp.cumsum(onehot, axis=0) - onehot
    position = jnp.sum(before * onehot, axis=1)
    return (flat_ids * capacity + position).reshape(length, pick_count)


def on_device(
    tokens,
    teacher_routes,
    teacher_share,
    student_routes,
    gate_weight,
    up_weight,
    down_weight,
    enc_weight,
    enc_bias,
    dec_weight,
):
    span_size = lax.axis_size("expert") // EXPERTS
    col_width = tokens.shape[1]
    full_width = col_width * lax.axis_size("tensor")
    teacher_slot = slot_table(teacher_routes, EXPERTS, CAP)
    slot_hits = (
        teacher_slot[:, :, None] == jnp.arange(EXPERTS * CAP, dtype=jnp.int32)[None, None, :]
    )
    spread = jnp.any(slot_hits, axis=1).astype(jnp.bfloat16)
    shares = jnp.stack([teacher_share, 1.0 - teacher_share], axis=1)
    weighting = jnp.sum(jnp.where(slot_hits, shares[:, :, None], 0.0), axis=1)
    full_tokens = lax.all_gather(tokens, "tensor", axis=1, tiled=True)
    packed = jnp.einsum(
        "tc,tw->cw", spread, full_tokens, preferred_element_type=jnp.float32
    ).astype(jnp.bfloat16)
    packed = packed.reshape(EXPERTS, CAP, full_tokens.shape[1])
    arrived = lax.all_to_all(
        jnp.repeat(packed, span_size, axis=0), "expert", split_axis=0, concat_axis=0, tiled=True
    )
    sources, slot_count, _ = arrived.shape
    flat_rows = arrived.reshape(sources * slot_count, full_width)
    gate_proj = jnp.dot(flat_rows, gate_weight[0], preferred_element_type=jnp.float32)
    up_proj = jnp.dot(flat_rows, up_weight[0], preferred_element_type=jnp.float32)
    hidden = (jax.nn.silu(gate_proj) * up_proj).astype(jnp.bfloat16)
    piece_cols = down_weight[0]
    summed_cols = lax.psum_scatter(
        lax.dot_general(
            piece_cols, hidden, (((0,), (1,)), ((), ())), preferred_element_type=jnp.float32
        ).astype(jnp.bfloat16),
        "tensor",
        scatter_dimension=0,
        tiled=True,
    ).astype(jnp.float32)
    back_rows = summed_cols.T.astype(jnp.bfloat16).reshape(sources, slot_count, col_width)
    returned = lax.all_to_all(back_rows, "expert", split_axis=0, concat_axis=0, tiled=True)
    summed = jnp.sum(
        returned.astype(jnp.float32).reshape(EXPERTS, span_size, CAP, col_width), axis=1
    ).reshape(EXPERTS * CAP, col_width)
    target = jnp.dot(
        weighting, summed, precision=lax.Precision.HIGHEST, preferred_element_type=jnp.float32
    )
    student_slot = slot_table(student_routes, DICTS, CAP_S)
    picked = student_slot[:, 0][:, None] == jnp.arange(DICTS * CAP_S, dtype=jnp.int32)[None, :]
    sending = picked.astype(jnp.bfloat16)
    selector = picked.astype(jnp.float32)
    outgoing = jnp.einsum("tc,tw->cw", sending, tokens, preferred_element_type=jnp.float32).astype(
        jnp.bfloat16
    )
    outgoing = jnp.repeat(outgoing.reshape(DICTS, CAP_S, col_width), span_size, axis=0)
    student_in = lax.all_to_all(outgoing, "expert", split_axis=0, concat_axis=0, tiled=True)
    sources = student_in.shape[0]
    inputs_full = student_in.reshape(sources * CAP_S, col_width).astype(jnp.float32)
    pre_part = jnp.dot(
        inputs_full,
        enc_weight[0],
        precision=lax.Precision.HIGHEST,
        preferred_element_type=jnp.float32,
    )
    pre_sum = lax.psum(pre_part, "tensor") + enc_bias[0][None, :]
    latent, gelu_back = jax.vjp(activation, pre_sum)
    partial_out = jnp.dot(
        latent, dec_weight[0], precision=lax.Precision.HIGHEST, preferred_element_type=jnp.float32
    )
    back_parts = lax.all_to_all(
        partial_out.reshape(sources, CAP_S, col_width),
        "expert",
        split_axis=0,
        concat_axis=0,
        tiled=True,
    )
    estimate = jnp.sum(back_parts.reshape(DICTS, span_size, CAP_S, col_width), axis=1).reshape(
        DICTS * CAP_S, col_width
    )
    predicted = jnp.dot(
        selector, estimate, precision=lax.Precision.HIGHEST, preferred_element_type=jnp.float32
    )
    error_rows = (predicted - target) * error_scale
    error_slots = lax.dot_general(
        selector,
        error_rows,
        (((0,), (0,)), ((), ())),
        precision=lax.Precision.HIGHEST,
        preferred_element_type=jnp.float32,
    )
    error_slots = jnp.repeat(error_slots.reshape(DICTS, CAP_S, col_width), span_size, axis=0)
    error_back = lax.all_to_all(error_slots, "expert", split_axis=0, concat_axis=0, tiled=True)
    error_flat = error_back.reshape(sources * CAP_S, col_width)
    dec_grad = lax.dot_general(
        latent,
        error_flat,
        (((0,), (0,)), ((), ())),
        precision=lax.Precision.HIGHEST,
        preferred_element_type=jnp.float32,
    )
    latent_part = lax.dot_general(
        error_flat,
        dec_weight[0],
        (((1,), (1,)), ((), ())),
        precision=lax.Precision.HIGHEST,
        preferred_element_type=jnp.float32,
    )
    latent_sum = lax.psum(latent_part, "tensor")
    pre_grad = gelu_back(latent_sum)[0]
    enc_grad = lax.dot_general(
        inputs_full,
        pre_grad,
        (((0,), (0,)), ((), ())),
        precision=lax.Precision.HIGHEST,
        preferred_element_type=jnp.float32,
    )
    bias_grad = jnp.sum(pre_grad, axis=0)
    return (enc_grad[None], bias_grad[None], dec_grad[None])


def solution(mesh):
    return jax.shard_map(
        on_device,
        mesh=mesh,
        in_specs=(
            P(("groups", "expert"), "tensor"),
            P(("groups", "expert"), None),
            P(("groups", "expert")),
            P(("groups", "expert"), None),
            P("expert", None, "tensor"),
            P("expert", None, "tensor"),
            P("expert", "tensor", None),
            P("expert", "tensor", None),
            P("expert", None),
            P("expert", None, "tensor"),
        ),
        out_specs=(
            P(("groups", "expert"), "tensor", None),
            P(("groups", "expert"), None),
            P(("groups", "expert"), None, "tensor"),
        ),
        check_vma=False,
    )
```

profile of v0, /device:TPU:0, one launch (start us, length us, event | category | flops | bytes accessed | tf_op | source)
XLA Modules:
  0.0 404.2 jit_solution(6848395262997627204)
XLA Ops:
  7.2 0.7 fusion.39
  8.1 0.8 select_reduce_fusion.1
  9.6 2.0 convolution_convert_fusion.1
  11.6 4.2 %all-to-all-start = ((bf16[4,48,768]{2,1,0:T(8,128)(2,1)}), bf16[4,48,768]{2,1,0:T(8,128)(2,1)S(1)}, u32[]{:S(2)}, u32[]{:S(2)}) async-start(bf16[4,48,768]{2,1,0:T(8,128)(2,1)} %bitcast.3), calls=%async_computation | async-start | bytes 589824 | tf_op jit(solution)/shard_map/all_to_all | solution.py:90
  15.8 0.8 copy.31
  16.9 20.7 %all_gather.3 = bf16[128,3072]{1,0:T(8,128)(2,1)S(1)} all-gather(bf16[128,768]{1,0:T(8,128)(2,1)} %param.10), channel_id=1, replica_groups=mesh['groups'=2,'expert'=4,'tensor'=4] {'tensor'}, dimensions={1}, use_global_device_ids=true | all-gather | bytes 983040 | tf_op jit(solution)/shard_map/all_gather | solution.py:52
  37.6 1.2 reduce-window.6
  39.4 0.7 multiply_add_fusion
  40.2 1.9 convolution_convert_fusion
  42.1 3.6 all-to-all-start.2
  45.8 10.7 %fusion.10 = f32[192,4096]{1,0:T(8,128)} fusion(bf16[192,768]{1,0:T(8,128)(2,1)S(1)} %bitcast.96, f32[1,768,4096]{2,1,0:T(8,128)} %param.17), kind=kOutput, calls=%fused_computation.10 | convolution fusion | flops 7247757312 | bytes 16023552 | tf_op jit(solution)/shard_map/dot_general | solution.py:93
  56.7 13.3 %all-to-all-done.2 = bf16[4,80,3072]{2,1,0:T(8,128)(2,1)S(1)} async-done(((bf16[4,80,3072]{2,1,0:T(8,128)(2,1)}), bf16[4,80,3072]{2,1,0:T(8,128)(2,1)S(1)}, u32[]{:S(2)}, u32[]{:S(2)}) %all-to-all-start.2) | async-done | bytes 1966112 | tf_op jit(solution)/shard_map/all_to_all | solution.py:57
  70.0 8.8 %fusion.4 = f32[320,2048]{1,0:T(8,128)} fusion(bf16[320,3072]{1,0:T(8,128)(2,1)S(1)} %bitcast.99, bf16[1,3072,2048]{2,1,0:T(8,128)(2,1)} %param.14), kind=kOutput, calls=%fused_computation.4 | convolution fusion | flops 4026531840 | bytes 17170432 | tf_op jit(solution)/shard_map/dot_general | solution.py:62
  78.8 18.9 %fusion.15 = bf16[3072,320]{0,1:T(8,128)(2,1)} fusion(bf16[1,2048,3072]{2,1,0:T(8,128)(2,1)} %param.16, bf16[320,3072]{1,0:T(8,128)(2,1)S(1)} %bitcast.100, bf16[1,3072,2048]{2,1,0:T(8,128)(2,1)} %param.15, f32[320,2048]{1,0:T(8,128)} %fusion.4), kind=kOutput, calls=%fused_computation.18 | convolution fusion | flops 8057978880 | bytes 31719424 | tf_op jit(solution)/shard_map/dot_general | solution.py:67
  97.6 80.1 %all-reduce.3.cloned.1.call-done = f32[192,4096]{1,0:T(8,128)} async-done(((f32[192,4096]{1,0:T(8,128)}), f32[192,4096]{1,0:T(8,128)}) %all-reduce.3.cloned.1.call-update) | async-done | bytes 3145744 | tf_op jit(solution)/shard_map/psum | solution.py:99
  177.7 2.9 multiply_multiply_fusion.2
  180.7 12.6 %fusion.6 = f32[4,48,768]{2,1,0:T(8,128)} fusion(f32[4,48,4096]{2,1,0:T(8,128)S(1)} %bitcast.93, f32[1,4096,768]{2,1,0:T(8,128)} %param.19), kind=kOutput, calls=%fused_computation.6 | convolution fusion | flops 7247757312 | bytes 16318464 | tf_op jit(solution)/shard_map/dot_general | solution.py:101
  193.2 4.2 %all-to-all-start.1 = ((f32[4,48,768]{2,1,0:T(8,128)}), f32[4,48,768]{2,1,0:T(8,128)}, u32[]{:S(2)}, u32[]{:S(2)}) async-start(f32[4,48,768]{2,1,0:T(8,128)} %fusion.6), calls=%async_computation.1 | async-start | bytes 1179648 | tf_op jit(solution)/shard_map/all_to_all | solution.py:104
  197.4 9.6 %all-to-all-done.1 = f32[4,48,768]{2,1,0:T(8,128)} async-done(((f32[4,48,768]{2,1,0:T(8,128)}), f32[4,48,768]{2,1,0:T(8,128)}, u32[]{:S(2)}, u32[]{:S(2)}) %all-to-all-start.1) | async-done | bytes 589856 | tf_op jit(solution)/shard_map/all_to_all | solution.py:104
  207.0 13.5 %reduce-scatter.2.cloned.1.call-done = bf16[768,320]{0,1:T(8,128)(2,1)} async-done(((bf16[3072,320]{0,1:T(8,128)(2,1)}), bf16[768,320]{0,1:T(8,128)(2,1)}) %reduce-scatter.2.cloned.1.call-update) | async-done | bytes 491536 | tf_op jit(solution)/shard_map/reduce_scatter | solution.py:66
  220.5 4.1 %all-to-all-start.3 = ((bf16[4,80,768]{2,1,0:T(8,128)(2,1)}), bf16[4,80,768]{2,1,0:T(8,128)(2,1)}, u32[]{:S(2)}, u32[]{:S(2)}) async-start(bf16[4,80,768]{2,1,0:T(8,128)(2,1)} %bitcast.101), calls=%async_computation.4 | async-start | bytes 983040 | tf_op jit(solution)/shard_map/all_to_all | solution.py:75
  224.7 0.7 select_reduce_fusion
  225.4 2.2 fusion.35
  227.6 5.6 %all-to-all-done.3 = bf16[4,80,768]{2,1,0:T(8,128)(2,1)} async-done(((bf16[4,80,768]{2,1,0:T(8,128)(2,1)}), bf16[4,80,768]{2,1,0:T(8,128)(2,1)}, u32[]{:S(2)}, u32[]{:S(2)}) %all-to-all-start.3) | async-done | bytes 491552 | tf_op jit(solution)/shard_map/all_to_all | solution.py:75
  233.2 1.8 fusion.30
  235.5 11.9 %all_to_all.25 = f32[4,48,768]{2,1,0:T(8,128)S(1)} all-to-all(f32[4,48,768]{2,1,0:T(8,128)S(1)} %bitcast.98), channel_id=1, replica_groups=mesh['groups'=2,'expert'=4,'tensor'=4] {'expert'}, dimensions={0} | all-to-all | bytes 1179648 | tf_op jit(solution)/shard_map/all_to_all | solution.py:126
  247.5 0.8 copy-done
  248.3 16.8 %fusion.8 = f32[192,4096]{1,0:T(8,128)} fusion(f32[192,768]{1,0:T(8,128)S(1)} %bitcast.94, f32[1,4096,768]{2,1,0:T(8,128)} %param.19), kind=kOutput, calls=%fused_computation.8 | convolution fusion | flops 7247757312 | bytes 16318464 | tf_op jit(solution)/shard_map/dot_general | solution.py:135
  265.1 23.1 %convolution_bitcast_fusion = f32[1,4096,768]{2,1,0:T(8,128)} fusion(f32[192,4096]{1,0:T(8,128)S(1)} %multiply_multiply_fusion.2, f32[192,768]{1,0:T(8,128)} %bitcast.95), kind=kOutput, calls=%fused_computation.12 | convolution fusion | flops 7247757312 | bytes 16318464 | tf_op jit(solution)/shard_map/dot_general | solution.py:128
  288.2 96.5 %all-reduce.5.cloned.1.call-done = f32[192,4096]{1,0:T(8,128)} async-done(((f32[192,4096]{1,0:T(8,128)}), f32[192,4096]{1,0:T(8,128)}) %all-reduce.5.cloned.1.call-update) | async-done | bytes 3145744 | tf_op jit(solution)/shard_map/psum | solution.py:142
  384.7 4.8 %fusion.45 = (f32[4096]{0:T(1024)}, f32[192,4096]{1,0:T(8,128)S(1)}) fusion(f32[192,4096]{1,0:T(8,128)} %all-reduce.5.cloned.1.call-done, f32[192,4096]{1,0:T(8,128)} %all-reduce.3.cloned.1.call-done, f32[4096]{0:T(1024)S(1)} %bitcast.103), kind=kLoop, calls=%fused_computation.56 | loop fusion | flops 16510976 | bytes 9469952 | tf_op jit(solution)/shard_map/reduce_sum | solution.py:151
  389.5 8.1 %convolution_bitcast_fusion.1 = f32[1,768,4096]{2,1,0:T(8,128)} fusion(bf16[192,768]{1,0:T(8,128)(2,1)S(1)} %bitcast.97, f32[192,4096]{1,0:T(8,128)S(1)} %get-tuple-element.4), kind=kOutput, calls=%fused_computation.13 | convolution fusion | flops 7247757312 | bytes 16023552 | tf_op jit(solution)/shard_map/dot_general | solution.py:144
  (30 shorter events, 2.7 us)
Async XLA Ops:
  11.6 30.5 %all-to-all-start = ((bf16[4,48,768]{2,1,0:T(8,128)(2,1)}), bf16[4,48,768]{2,1,0:T(8,128)(2,1)S(1)}, u32[]{:S(2)}, u32[]{:S(2)}) async-start(bf16[4,48,768]{2,1,0:T(8,128)(2,1)} %bitcast.3), calls=%async_computation | async-start | bytes 589824 | tf_op jit(solution)/shard_map/all_to_all | solution.py:90
  42.1 27.9 %all-to-all-start.2 = ((bf16[4,80,3072]{2,1,0:T(8,128)(2,1)}), bf16[4,80,3072]{2,1,0:T(8,128)(2,1)S(1)}, u32[]{:S(2)}, u32[]{:S(2)}) async-start(bf16[4,80,3072]{2,1,0:T(8,128)(2,1)} %bitcast.15), calls=%async_computation.2 | async-start | bytes 3932160 | tf_op jit(solution)/shard_map/all_to_all | solution.py:57
  45.7 132.0 %all-reduce.3.cloned.1.call-start = ((), (), s32[]{:S(2)}) async-start(), calls=%async_computation.6 | async-start | bytes 6291456 | tf_op jit(solution)/shard_map/psum | solution.py:99
  56.5 164.1 %reduce-scatter.2.cloned.1.call-start = ((), (), s32[]{:S(2)}) async-start(), calls=%async_computation.7 | async-start | bytes 2457600 | tf_op jit(solution)/shard_map/reduce_scatter | solution.py:66
  78.8 99.0 %copy-start.1 = (f32[1,4096]{1,0:T(1,128)S(1)}, f32[1,4096]{1,0:T(1,128)}, u32[]{:S(2)}) copy-start(f32[1,4096]{1,0:T(1,128)} %param.18) | copy-start | bytes 49156
  180.6 16.8 %copy-start.2 = (f32[128]{0:T(128)S(1)}, f32[128]{0:T(128)}, u32[]{:S(2)}) copy-start(f32[128]{0:T(128)} %param.12) | copy-start | bytes 1540
  193.2 13.8 %all-to-all-start.1 = ((f32[4,48,768]{2,1,0:T(8,128)}), f32[4,48,768]{2,1,0:T(8,128)}, u32[]{:S(2)}, u32[]{:S(2)}) async-start(f32[4,48,768]{2,1,0:T(8,128)} %fusion.6), calls=%async_computation.1 | async-start | bytes 1179648 | tf_op jit(solution)/shard_map/all_to_all | solution.py:104
  220.5 12.7 %all-to-all-start.3 = ((bf16[4,80,768]{2,1,0:T(8,128)(2,1)}), bf16[4,80,768]{2,1,0:T(8,128)(2,1)}, u32[]{:S(2)}, u32[]{:S(2)}) async-start(bf16[4,80,768]{2,1,0:T(8,128)(2,1)} %bitcast.101), calls=%async_computation.4 | async-start | bytes 983040 | tf_op jit(solution)/shard_map/all_to_all | solution.py:75
  224.7 160.0 %all-reduce.5.cloned.1.call-start = ((), (), s32[]{:S(2)}) async-start(), calls=%async_computation.8 | async-start | bytes 6291456 | tf_op jit(solution)/shard_map/psum | solution.py:142
  247.5 0.8 copy-start
Sparse Core Ops, SparseCore 0:
  56.6 121.0 all-reduce.2
  180.0 40.4 reduce-scatter.1
  265.2 119.3 all-reduce.4
where the time goes:
time: 405 us; the launch traced here: 404 us
  waiting for transfers between devices  219 us (54%)
  matrix products  107 us (26%)
  blocking collectives  32.6 us (8%)
  starting transfers between devices  16.4 us (4%)
  between operations  13.9 us (3%)
  other arithmetic  13 us (3%)
    psum x1, waiting for transfers between devices, on_device(): latent_sum = lax.psum(latent_part, 'tensor')  96.5 us
    psum x1, waiting for transfers between devices, on_device(): pre_sum = lax.psum(pre_part, 'tensor') + enc_bias[0][None, :]  80.1 us
    dot_general x1, matrix products, on_device(): lax.dot_general(latent, error_flat, (((0,), (0,)), ((), ())), precision=l...  23.1 us
    all_gather x1, blocking collectives, on_device(): full_tokens = lax.all_gather(tokens, 'tensor', axis=1, tiled=True)  20.7 us
    dot_general x1, matrix products, on_device(): lax.dot_general(piece_cols, hidden, (((0,), (1,)), ((), ())), preferred_e...  18.9 us
    dot_general x1, matrix products, on_device(): lax.dot_general(error_flat, dec_weight[0], (((1,), (1,)), ((), ())), prec...  16.8 us
    reduce_scatter x1, waiting for transfers between devices, on_device(): lax.psum_scatter(lax.dot_general(piece_cols, hidden, (((0,), (1,)), ((),...  13.5 us
    all_to_all x1, waiting for transfers between devices, on_device(): lax.all_to_all(jnp.repeat(packed, span_size, axis=0), 'expert', split_axi...  13.3 us
  transfers between devices with their start and end apart: 7, of which 6 were waited for; matrix products, arithmetic and copies ran while one was open for 21% of the time, Pallas kernels for 0%

commit v1 on v0

--- a/solution.py
+++ b/solution.py
@@ -62,22 +62,22 @@
     gate_proj = jnp.dot(flat_rows, gate_weight[0], preferred_element_type=jnp.float32)
     up_proj = jnp.dot(flat_rows, up_weight[0], preferred_element_type=jnp.float32)
     hidden = (jax.nn.silu(gate_proj) * up_proj).astype(jnp.bfloat16)
-    piece_cols = down_weight[0]
-    summed_cols = lax.psum_scatter(
-        lax.dot_general(
-            piece_cols, hidden, (((0,), (1,)), ((), ())), preferred_element_type=jnp.float32
-        ).astype(jnp.bfloat16),
-        "tensor",
-        scatter_dimension=0,
-        tiled=True,
-    ).astype(jnp.float32)
-    back_rows = summed_cols.T.astype(jnp.bfloat16).reshape(sources, slot_count, col_width)
-    returned = lax.all_to_all(back_rows, "expert", split_axis=0, concat_axis=0, tiled=True)
+    part_rows = jnp.dot(hidden, down_weight[0], preferred_element_type=jnp.float32)
+    part_rows = part_rows.astype(jnp.bfloat16).reshape(sources, slot_count, full_width)
+    returned = lax.all_to_all(part_rows, "expert", split_axis=0, concat_axis=0, tiled=True)
     summed = jnp.sum(
-        returned.astype(jnp.float32).reshape(EXPERTS, span_size, CAP, col_width), axis=1
-    ).reshape(EXPERTS * CAP, col_width)
-    target = jnp.dot(
-        weighting, summed, precision=lax.Precision.HIGHEST, preferred_element_type=jnp.float32
+        returned.astype(jnp.float32).reshape(EXPERTS, span_size, CAP, full_width), axis=1
+    ).reshape(EXPERTS * CAP, full_width)
+    mixed = jnp.dot(
+        weighting, summed, precision=lax.Precision.HIGH, preferred_element_type=jnp.float32
+    ).astype(jnp.bfloat16)
+    tensor_size = lax.axis_size("tensor")
+    token_count = mixed.shape[0]
+    mixed = mixed.reshape(token_count, tensor_size, col_width).transpose(1, 0, 2)
+    target = (
+        lax.psum_scatter(mixed, "tensor", scatter_dimension=0, tiled=True)
+        .reshape(token_count, col_width)
+        .astype(jnp.float32)
     )
     student_slot = slot_table(student_routes, DICTS, CAP_S)
     picked = student_slot[:, 0][:, None] == jnp.arange(DICTS * CAP_S, dtype=jnp.int32)[None, :]
@@ -89,17 +89,36 @@
     outgoing = jnp.repeat(outgoing.reshape(DICTS, CAP_S, col_width), span_size, axis=0)
     student_in = lax.all_to_all(outgoing, "expert", split_axis=0, concat_axis=0, tiled=True)
     sources = student_in.shape[0]
-    inputs_full = student_in.reshape(sources * CAP_S, col_width).astype(jnp.float32)
+    rows = sources * CAP_S
+    inputs_flat = student_in.reshape(rows, col_width)
     pre_part = jnp.dot(
-        inputs_full,
+        inputs_flat.astype(jnp.float32),
         enc_weight[0],
-        precision=lax.Precision.HIGHEST,
+        precision=lax.Precision.HIGH,
         preferred_element_type=jnp.float32,
     )
-    pre_sum = lax.psum(pre_part, "tensor") + enc_bias[0][None, :]
-    latent, gelu_back = jax.vjp(activation, pre_sum)
+    lat_size = pre_part.shape[1]
+    lat_cols = lat_size // tensor_size
+
+    def scatter_latents(part):
+        blocks = part.reshape(rows, tensor_size, lat_cols).transpose(1, 0, 2)
+        own = lax.psum_scatter(blocks, "tensor", scatter_dimension=0, tiled=True)
+        return own.reshape(rows, lat_cols)
+
+    def gather_latents(own):
+        blocks = lax.all_gather(own.astype(jnp.bfloat16), "tensor", axis=0, tiled=False)
+        return blocks.transpose(1, 0, 2).reshape(rows, lat_size)
+
+    bias_own = lax.dynamic_slice_in_dim(
+        enc_bias[0], lax.axis_index("tensor") * lat_cols, lat_cols
+    )
+    pre_own = scatter_latents(pre_part) + bias_own[None, :]
+    latent_own, gelu_back = jax.vjp(activation, pre_own)
+    latent = gather_latents(latent_own)
     partial_out = jnp.dot(
-        latent, dec_weight[0], precision=lax.Precision.HIGHEST, preferred_element_type=jnp.float32
+        latent,
+        dec_weight[0].astype(jnp.bfloat16),
+        preferred_element_type=jnp.float32,
     )
     back_parts = lax.all_to_all(
         partial_out.reshape(sources, CAP_S, col_width),
@@ -124,31 +143,29 @@
     )
     error_slots = jnp.repeat(error_slots.reshape(DICTS, CAP_S, col_width), span_size, axis=0)
     error_back = lax.all_to_all(error_slots, "expert", split_axis=0, concat_axis=0, tiled=True)
-    error_flat = error_back.reshape(sources * CAP_S, col_width)
-    dec_grad = lax.dot_general(
-        latent,
-        error_flat,
-        (((0,), (0,)), ((), ())),
-        precision=lax.Precision.HIGHEST,
-        preferred_element_type=jnp.float32,
-    )
+    error_flat = error_back.reshape(rows, col_width)
     latent_part = lax.dot_general(
         error_flat,
         dec_weight[0],
         (((1,), (1,)), ((), ())),
-        precision=lax.Precision.HIGHEST,
+        precision=lax.Precision.HIGH,
         preferred_element_type=jnp.float32,
     )
-    latent_sum = lax.psum(latent_part, "tensor")
-    pre_grad = gelu_back(latent_sum)[0]
+    latent_sum = scatter_latents(latent_part)
+    dec_grad = lax.dot_general(
+        latent,
+        error_flat.astype(jnp.bfloat16),
+        (((0,), (0,)), ((), ())),
+        preferred_element_type=jnp.float32,
+    )
+    pre_grad = gather_latents(gelu_back(latent_sum)[0])
     enc_grad = lax.dot_general(
-        inputs_full,
+        inputs_flat,
         pre_grad,
         (((0,), (0,)), ((), ())),
-        precision=lax.Precision.HIGHEST,
         preferred_element_type=jnp.float32,
     )
-    bias_grad = jnp.sum(pre_grad, axis=0)
+    bias_grad = jnp.sum(pre_grad.astype(jnp.float32), axis=0)
     return (enc_grad[None], bias_grad[None], dec_grad[None])
 
 

time: 405 us -> 330 us (0.81)
  waiting for transfers between devices: 219 us -> 150 us
  matrix products: 107 us -> 76.5 us
  local copies, waits for them, and re-layouts: 2.36 us -> 19.8 us
  blocking collectives: 32.6 us -> 42.8 us
    psum x2 -> x0, waiting for transfers between devices: 177 us -> none  [the longest x1 96.5 us: on_device(): latent_sum = lax.psum(latent_part, 'tensor')]
    reduce_scatter x1 -> x3, waiting for transfers between devices: 13.5 us -> 71.5 us  [the longest x2 61.2 us: scatter_latents(): own = lax.psum_scatter(blocks, 'tensor', scatter_dimension=0, tiled=True)]
    all_gather x0 -> x2, waiting for transfers between devices: none -> 30.4 us  [gather_latents(): lax.all_gather(own.astype(jnp.bfloat16), 'tensor', axis=0, tiled=False)]
    dot_general x6, matrix products: 75.1 us -> 50.5 us  [the longest x1 18.8 us: on_device(): jnp.dot(hidden, down_weight[0], preferred_element_type=jnp.float32)]
    all_to_all x1, waiting for transfers between devices: 5.6 us -> 23.9 us  [on_device(): lax.all_to_all(part_rows, 'expert', split_axis=0, concat_axis=0, tiled=True)]
    dot_general x0 -> x2, local copies, waits for them, and re-layouts: none -> 13.8 us  [the longest x1 12.6 us: on_device(): jnp.dot(inputs_flat.astype(jnp.float32), enc_weight[0], precision=lax.Pre...]
    all_to_all x1, waiting for transfers between devices: 13.3 us -> 24 us  [on_device(): lax.all_to_all(jnp.repeat(packed, span_size, axis=0), 'expert', split_axi...]
    all_gather x1, blocking collectives: 20.7 us -> 30.8 us  [on_device(): full_tokens = lax.all_gather(tokens, 'tensor', axis=1, tiled=True)]
  transfers between devices with their start and end apart: 7 -> 9, of which waited for: 6 -> 6; matrix products, arithmetic and copies ran while one was open for 21% -> 19% of each run, Pallas kernels for 0% -> 0%
where the time goes in v1:
time: 330 us; the launch traced here: 329 us
  waiting for transfers between devices  150 us (45%)
  matrix products  76.5 us (23%)
  blocking collectives  42.8 us (13%)
  local copies, waits for them, and re-layouts  19.8 us (6%)
  starting transfers between devices  15.8 us (5%)
  between operations  14 us (4%)
  other arithmetic  10.3 us (3%)
    reduce_scatter x2, waiting for transfers between devices, scatter_latents(): own = lax.psum_scatter(blocks, 'tensor', scatter_dimension=0, tiled=True)  61.2 us
    all_gather x1, blocking collectives, on_device(): full_tokens = lax.all_gather(tokens, 'tensor', axis=1, tiled=True)  30.8 us
    all_gather x2, waiting for transfers between devices, gather_latents(): lax.all_gather(own.astype(jnp.bfloat16), 'tensor', axis=0, tiled=False)  30.4 us
    all_to_all x1, waiting for transfers between devices, on_device(): lax.all_to_all(jnp.repeat(packed, span_size, axis=0), 'expert', split_axi...  24 us
    all_to_all x1, waiting for transfers between devices, on_device(): lax.all_to_all(part_rows, 'expert', split_axis=0, concat_axis=0, tiled=True)  23.9 us
    dot_general x1, matrix products, on_device(): jnp.dot(hidden, down_weight[0], preferred_element_type=jnp.float32)  18.8 us
    dot_general x1, local copies, waits for them, and re-layouts, on_device(): jnp.dot(inputs_flat.astype(jnp.float32), enc_weight[0], precision=lax.Pre...  12.6 us
    all_to_all x1, blocking collectives, on_device(): lax.all_to_all(error_slots, 'expert', split_axis=0, concat_axis=0, tiled=...  12.1 us
  transfers between devices with their start and end apart: 9, of which 6 were waited for; matrix products, arithmetic and copies ran while one was open for 19% of the time, Pallas kernels for 0%

profile of v1, /device:TPU:0, one launch (start us, length us, event | category | flops | bytes accessed | tf_op | source)
XLA Modules:
  0.0 329.2 jit_solution(3863646675823719374)
XLA Ops:
  8.1 0.8 select_reduce_fusion.1
  9.6 2.0 convolution_convert_fusion.2
  11.6 4.2 %all-to-all-start = ((bf16[4,48,768]{2,1,0:T(8,128)(2,1)}), bf16[4,48,768]{2,1,0:T(8,128)(2,1)S(1)}, u32[]{:S(2)}, u32[]{:S(2)}) async-start(bf16[4,48,768]{2,1,0:T(8,128)(2,1)} %bitcast.3), calls=%async_computation | async-start | bytes 589824 | tf_op jit(solution)/shard_map/all_to_all | solution.py:90
  15.8 12.6 %copy.63 = f32[4096,768]{1,0:T(8,128)} copy(f32[4096,768]{0,1:T(8,128)} %bitcast.118) | data formatting | bytes 25165824 | tf_op jit(solution)/shard_map/dot_general | solution.py:94
  28.4 10.5 %convolution_bitcast_fusion.3 = f32[4,192,1024]{2,1,0:T(8,128)} fusion(bf16[192,768,1]{1,0,2:T(8,128)(2,1)S(1)} %bitcast.128, f32[4,1024,768]{2,1,0:T(8,128)} %bitcast.117), kind=kOutput, calls=%fused_computation.18 | convolution fusion | flops 3623878656 | bytes 16023552 | tf_op jit(solution)/shard_map/dot_general | solution.py:94
  40.0 1.2 reduce-window.6
  41.9 30.8 %all_gather.12 = bf16[128,3072]{1,0:T(8,128)(2,1)S(1)} all-gather(bf16[128,768]{1,0:T(8,128)(2,1)S(1)} %copy-done.5), channel_id=1, replica_groups=mesh['groups'=2,'expert'=4,'tensor'=4] {'tensor'}, dimensions={1}, use_global_device_ids=true | all-gather | bytes 983040 | tf_op jit(solution)/shard_map/all_gather | solution.py:52
  72.7 1.9 convolution_convert_fusion
  74.6 3.6 %all-to-all-start.2 = ((bf16[4,80,3072]{2,1,0:T(8,128)(2,1)}), bf16[4,80,3072]{2,1,0:T(8,128)(2,1)S(1)}, u32[]{:S(2)}, u32[]{:S(2)}) async-start(bf16[4,80,3072]{2,1,0:T(8,128)(2,1)} %bitcast.19), calls=%async_computation.3 | async-start | bytes 3932160 | tf_op jit(solution)/shard_map/all_to_all | solution.py:57
  78.5 24.0 %all-to-all-done.2 = bf16[4,80,3072]{2,1,0:T(8,128)(2,1)S(1)} async-done(((bf16[4,80,3072]{2,1,0:T(8,128)(2,1)}), bf16[4,80,3072]{2,1,0:T(8,128)(2,1)S(1)}, u32[]{:S(2)}, u32[]{:S(2)}) %all-to-all-start.2) | async-done | bytes 1966112 | tf_op jit(solution)/shard_map/all_to_all | solution.py:57
  102.5 8.8 %fusion.4 = f32[320,2048]{1,0:T(8,128)} fusion(bf16[320,3072]{1,0:T(8,128)(2,1)S(1)} %bitcast.132, bf16[1,3072,2048]{2,1,0:T(8,128)(2,1)} %param.14), kind=kOutput, calls=%fused_computation.4 | convolution fusion | flops 4026531840 | bytes 17170432 | tf_op jit(solution)/shard_map/dot_general | solution.py:62
  111.3 0.8 reduce-scatter.4.cloned.1.call-done
  112.1 2.2 multiply_convert_fusion
  114.3 18.8 %fusion.9 = bf16[320,3072]{1,0:T(8,128)(2,1)} fusion(bf16[1,2048,3072]{2,1,0:T(8,128)(2,1)} %param.16, bf16[320,3072]{1,0:T(8,128)(2,1)S(1)} %bitcast.133, bf16[1,3072,2048]{2,1,0:T(8,128)(2,1)} %param.15, f32[320,2048]{1,0:T(8,128)} %fusion.4), kind=kOutput, calls=%fused_computation.12 | convolution fusion | flops 8057978880 | bytes 31719424 | tf_op jit(solution)/shard_map/dot_general | solution.py:65
  133.0 3.7 %all-to-all-start.3 = ((bf16[4,80,3072]{2,1,0:T(8,128)(2,1)}), bf16[4,80,3072]{2,1,0:T(8,128)(2,1)S(1)}, u32[]{:S(2)}, u32[]{:S(2)}) async-start(bf16[4,80,3072]{2,1,0:T(8,128)(2,1)} %bitcast.134), calls=%async_computation.4 | async-start | bytes 3932160 | tf_op jit(solution)/shard_map/all_to_all | solution.py:67
  137.1 23.9 %all-to-all-done.3 = bf16[4,80,3072]{2,1,0:T(8,128)(2,1)S(1)} async-done(((bf16[4,80,3072]{2,1,0:T(8,128)(2,1)}), bf16[4,80,3072]{2,1,0:T(8,128)(2,1)S(1)}, u32[]{:S(2)}, u32[]{:S(2)}) %all-to-all-start.3) | async-done | bytes 1966112 | tf_op jit(solution)/shard_map/all_to_all | solution.py:67
  161.0 1.0 convolution_convert_fusion.1
  162.1 0.9 copy.71
  163.1 2.6 copy.54
  165.7 1.2 dot_general.51
  166.9 6.9 %fusion.6 = f32[4,48,768]{2,1,0:T(8,128)} fusion(bf16[4,48,4096]{2,1,0:T(8,128)(2,1)S(1)} %dot_general.51, f32[1,4096,768]{2,1,0:T(8,128)} %param.19), kind=kOutput, calls=%fused_computation.8 | convolution fusion | flops 1211105280 | bytes 14745600 | tf_op jit(solution)/shard_map/dot_general | solution.py:118
  173.8 3.5 %all-to-all-start.1 = ((f32[4,48,768]{2,1,0:T(8,128)}), f32[4,48,768]{2,1,0:T(8,128)S(1)}, u32[]{:S(2)}, u32[]{:S(2)}) async-start(f32[4,48,768]{2,1,0:T(8,128)} %fusion.6), calls=%async_computation.2 | async-start | bytes 1179648 | tf_op jit(solution)/shard_map/all_to_all | solution.py:123
  177.4 10.3 %reduce-scatter.6.cloned.1.call-done = bf16[1,128,768]{2,1,0:T(8,128)(2,1)} async-done(((bf16[4,128,768]{2,1,0:T(8,128)(2,1)}), bf16[1,128,768]{2,1,0:T(8,128)(2,1)}) %reduce-scatter.6.cloned.1.call-update) | async-done | bytes 196624 | tf_op jit(solution)/shard_map/reduce_scatter | solution.py:78
  187.7 1.3 fusion.18
  189.5 12.1 %all_to_all.25 = f32[4,48,768]{2,1,0:T(8,128)S(1)} all-to-all(f32[4,48,768]{2,1,0:T(8,128)S(1)} %bitcast.131), channel_id=1, replica_groups=mesh['groups'=2,'expert'=4,'tensor'=4] {'expert'}, dimensions={0} | all-to-all | bytes 1179648 | tf_op jit(solution)/shard_map/all_to_all | solution.py:145
  201.6 11.5 %convolution_bitcast_fusion.2 = f32[4,192,1024]{2,1,0:T(8,128)} fusion(f32[192,768,1]{1,0,2:T(8,128)S(1)} %bitcast.125, f32[4,1024,768]{2,1,0:T(8,128)} %bitcast.116), kind=kOutput, calls=%fused_computation.17 | convolution fusion | flops 3623878656 | bytes 16318464 | tf_op jit(solution)/shard_map/dot_general | solution.py:147
  213.4 60.3 %reduce-scatter.8.cloned.1.call-done = f32[1,192,1024]{2,1,0:T(8,128)} async-done(((f32[4,192,1024]{2,1,0:T(8,128)}), f32[1,192,1024]{2,1,0:T(8,128)}) %reduce-scatter.8.cloned.1.call-update) | async-done | bytes 786448 | tf_op jit(solution)/shard_map/reduce_scatter | solution.py:105
  273.8 2.4 fusion.25
  276.4 6.7 %convolution_bitcast_fusion = f32[1,4096,768]{2,1,0:T(8,128)} fusion(bf16[192,4096]{1,0:T(8,128)(2,1)S(1)} %bitcast.120, bf16[192,768]{1,0:T(8,128)(2,1)S(1)} %bitcast.135), kind=kOutput, calls=%fused_computation.6 | convolution fusion | flops 1207959552 | bytes 14450688 | tf_op jit(solution)/shard_map/dot_general | solution.py:155
  283.1 30.4 %all-gather.5.cloned.1.call-done = bf16[4,192,1024]{2,1,0:T(8,128)(2,1)} async-done(((bf16[1,192,1024]{2,1,0:T(8,128)(2,1)}), bf16[4,192,1024]{2,1,0:T(8,128)(2,1)}) %all-gather.5.cloned.1.call-update) | async-done | bytes 1572880 | tf_op jit(solution)/shard_map/all_gather | solution.py:109
  313.5 1.8 convert_reduce_fusion
  316.1 6.6 %convolution_bitcast_fusion.1 = f32[1,768,4096]{2,1,0:T(8,128)} fusion(bf16[192,768]{1,0:T(8,128)(2,1)S(1)} %bitcast.129, bf16[192,4096]{1,0:T(8,128)(2,1)S(1)} %bitcast.124), kind=kOutput, calls=%fused_computation.7 | convolution fusion | flops 1207959552 | bytes 14450688 | tf_op jit(solution)/shard_map/dot_general | solution.py:162
  (56 shorter events, 5.8 us)
Async XLA Ops:
  7.2 71.3 %copy-start = (f32[1,4096]{1,0:T(1,128)S(1)}, f32[1,4096]{1,0:T(1,128)}, u32[]{:S(2)}) copy-start(f32[1,4096]{1,0:T(1,128)} %param.18) | copy-start | bytes 49156
  11.6 16.8 %all-to-all-start = ((bf16[4,48,768]{2,1,0:T(8,128)(2,1)}), bf16[4,48,768]{2,1,0:T(8,128)(2,1)S(1)}, u32[]{:S(2)}, u32[]{:S(2)}) async-start(bf16[4,48,768]{2,1,0:T(8,128)(2,1)} %bitcast.3), calls=%async_computation | async-start | bytes 589824 | tf_op jit(solution)/shard_map/all_to_all | solution.py:90
  15.8 96.3 %reduce-scatter.4.cloned.1.call-start = ((), (), s32[]{:S(2)}) async-start(), calls=%async_computation.8 | async-start | bytes 3932160 | tf_op jit(solution)/shard_map/reduce_scatter | solution.py:105
  38.9 0.7 copy-start.6
  38.9 3.0 copy-start.5
  74.6 27.9 %all-to-all-start.2 = ((bf16[4,80,3072]{2,1,0:T(8,128)(2,1)}), bf16[4,80,3072]{2,1,0:T(8,128)(2,1)S(1)}, u32[]{:S(2)}, u32[]{:S(2)}) async-start(bf16[4,80,3072]{2,1,0:T(8,128)(2,1)} %bitcast.19), calls=%async_computation.3 | async-start | bytes 3932160 | tf_op jit(solution)/shard_map/all_to_all | solution.py:57
  78.2 84.8 %all-gather.3.cloned.1.call-start = ((), (), s32[]{:S(2)}) async-start(), calls=%async_computation.9 | async-start | bytes 1966080 | tf_op jit(solution)/shard_map/all_gather | solution.py:109
  133.0 4.0 %copy-start.7 = (f32[128]{0:T(128)S(1)}, f32[128]{0:T(128)}, u32[]{:S(2)}) copy-start(f32[128]{0:T(128)} %param.12) | copy-start | bytes 1540
  133.0 28.0 %all-to-all-start.3 = ((bf16[4,80,3072]{2,1,0:T(8,128)(2,1)}), bf16[4,80,3072]{2,1,0:T(8,128)(2,1)S(1)}, u32[]{:S(2)}, u32[]{:S(2)}) async-start(bf16[4,80,3072]{2,1,0:T(8,128)(2,1)} %bitcast.134), calls=%async_computation.4 | async-start | bytes 3932160 | tf_op jit(solution)/shard_map/all_to_all | solution.py:67
  136.8 50.9 %reduce-scatter.6.cloned.1.call-start = ((), (), s32[]{:S(2)}) async-start(), calls=%async_computation.10 | async-start | bytes 983040 | tf_op jit(solution)/shard_map/reduce_scatter | solution.py:78
  173.8 13.9 %all-to-all-start.1 = ((f32[4,48,768]{2,1,0:T(8,128)}), f32[4,48,768]{2,1,0:T(8,128)S(1)}, u32[]{:S(2)}, u32[]{:S(2)}) async-start(f32[4,48,768]{2,1,0:T(8,128)} %fusion.6), calls=%async_computation.2 | async-start | bytes 1179648 | tf_op jit(solution)/shard_map/all_to_all | solution.py:123
  177.3 96.5 %reduce-scatter.8.cloned.1.call-start = ((), (), s32[]{:S(2)}) async-start(), calls=%async_computation.11 | async-start | bytes 3932160 | tf_op jit(solution)/shard_map/reduce_scatter | solution.py:105
  213.1 60.7 %copy-start.4 = (f32[1,192,1024]{2,1,0:T(8,128)S(1)}, f32[1,192,1024]{2,1,0:T(8,128)}, u32[]{:S(2)}) copy-start(f32[1,192,1024]{2,1,0:T(8,128)} %reduce-scatter.4.cloned.1.call-done) | copy-start | bytes 2359300
  213.1 63.1 %copy-start.2 = (bf16[4,192,1024]{2,1,0:T(8,128)(2,1)S(1)}, bf16[4,192,1024]{2,1,0:T(8,128)(2,1)}, u32[]{:S(2)}) copy-start(bf16[4,192,1024]{2,1,0:T(8,128)(2,1)} %all-gather.3.cloned.1.call-done) | copy-start | bytes 4718596
  213.1 100.4 %all-gather.5.cloned.1.call-start = ((), (), s32[]{:S(2)}) async-start(), calls=%async_computation.12 | async-start | bytes 1966080 | tf_op jit(solution)/shard_map/all_gather | solution.py:109
  313.5 2.5 copy-start.3
  316.1 6.6 %copy-start.1 = (f32[1,4096]{1,0:T(1,128)S(1)}, f32[1,4096]{1,0:T(1,128)}, u32[]{:S(2)}) copy-start(f32[1,4096]{1,0:T(1,128)} %param.18) | copy-start | bytes 49156
Sparse Core Ops, SparseCore 0:
  39.0 73.0 reduce-scatter.3
  114.4 39.1 all-gather.2
  163.1 24.4 reduce-scatter.5
  213.3 60.4 reduce-scatter.7
  276.3 37.1 all-gather.4

commit v2 on v1

--- a/solution.py
+++ b/solution.py
@@ -1,6 +1,11 @@
+import functools
+import math
+
 import jax
 import jax.numpy as jnp
 from jax import lax
+from jax.experimental import pallas as pl
+from jax.experimental.pallas import tpu as pltpu
 from jax.sharding import PartitionSpec as P
 
 EXPERTS = 4
@@ -12,8 +17,168 @@
 error_scale = 0.0625
 
 
-def activation(values):
-    return jax.nn.gelu(values, approximate=True)
+PIECES = 4
+BLOCK = 16
+ROOT = math.sqrt(2.0 / math.pi)
+MESH_IDS = pl.DeviceIdType.MESH
+
+
+def gelu_tail(v):
+    return jnp.tanh(ROOT * (v + 0.044715 * (v * v * v)))
+
+
+def exchange_kernel(
+    n, backward, part_ref, aux_ref, out_ref, *rest
+):
+    if backward:
+        own_ref = None
+        send32, recv32, send16, recv16, s32, r32, s16, r16, sg, rg = rest
+    else:
+        own_ref, send32, recv32, send16, recv16, s32, r32, s16, r16, sg, rg = rest
+    rows, cols = recv32.shape
+    piece = rows // PIECES
+    me = lax.axis_index("tensor")
+    pair, bit = me // 2, me % 2
+    partner = 2 * pair + 1 - bit
+    others = []
+    for q in range(1, n // 2):
+        for c in range(2):
+            others.append(2 * ((pair + q) % (n // 2)) + c)
+
+    def columns(index):
+        return pl.ds(pl.multiple_of(index * cols, cols), cols)
+
+    barrier = pltpu.get_barrier_semaphore()
+    for peer in [partner] + others:
+        pl.semaphore_signal(barrier, inc=1, device_id={"tensor": peer}, device_id_type=MESH_IDS)
+    pl.semaphore_wait(barrier, n - 1)
+
+    sends = []
+    for h in range(PIECES):
+        span = pl.ds(h * piece, piece)
+        for i, peer in enumerate(others):
+
+            @pl.loop(0, piece // BLOCK)
+            def _(j):
+                r = pl.ds(pl.multiple_of(h * piece + j * BLOCK, BLOCK), BLOCK)
+                send16[i, r, :] = part_ref[r, columns(peer)].astype(jnp.bfloat16)
+
+            copy = pltpu.make_async_remote_copy(
+                src_ref=send16.at[i, span],
+                dst_ref=recv16.at[me, span],
+                send_sem=s16.at[h, i],
+                recv_sem=r16.at[h, me],
+                device_id={"tensor": peer},
+                device_id_type=MESH_IDS,
+            )
+            copy.start()
+            sends.append(copy)
+
+        @pl.loop(0, piece // BLOCK)
+        def _(j):
+            r = pl.ds(pl.multiple_of(h * piece + j * BLOCK, BLOCK), BLOCK)
+            send32[r, :] = part_ref[r, columns(partner)]
+
+        copy = pltpu.make_async_remote_copy(
+            src_ref=send32.at[span],
+            dst_ref=recv32.at[span],
+            send_sem=s32.at[h],
+            recv_sem=r32.at[h],
+            device_id={"tensor": partner},
+            device_id_type=MESH_IDS,
+        )
+        copy.start()
+        sends.append(copy)
+
+    def arrival(ref, sem, peer):
+        return pltpu.make_async_remote_copy(
+            src_ref=ref,
+            dst_ref=ref,
+            send_sem=sem,
+            recv_sem=sem,
+            device_id={"tensor": peer},
+            device_id_type=MESH_IDS,
+        )
+
+    for h in range(PIECES):
+        span = pl.ds(h * piece, piece)
+        arrival(recv32.at[span], r32.at[h], partner).wait_recv()
+        for peer in others:
+            arrival(recv16.at[peer, span], r16.at[h, peer], peer).wait_recv()
+
+        @pl.loop(0, piece // BLOCK)
+        def _(j):
+            r = pl.ds(pl.multiple_of(h * piece + j * BLOCK, BLOCK), BLOCK)
+            total = part_ref[r, columns(me)] + recv32[r, :]
+            for peer in others:
+                total = total + recv16[peer, r, :].astype(jnp.float32)
+            if backward:
+                v = aux_ref[r, :]
+                t = gelu_tail(v)
+                slope = 0.5 * (1.0 + t) + (0.5 * ROOT) * v * (1.0 - t * t) * (
+                    1.0 + (3.0 * 0.044715) * (v * v)
+                )
+                value = total * slope
+            else:
+                v = total + aux_ref[:, columns(me)]
+                own_ref[r, :] = v
+                value = 0.5 * v * (1.0 + gelu_tail(v))
+            out_ref[r, columns(me)] = value.astype(jnp.bfloat16)
+
+        for i, peer in enumerate([partner] + others):
+            copy = pltpu.make_async_remote_copy(
+                src_ref=out_ref.at[span, columns(me)],
+                dst_ref=out_ref.at[span, columns(me)],
+                send_sem=sg.at[h, i],
+                recv_sem=rg.at[h, me],
+                device_id={"tensor": peer},
+                device_id_type=MESH_IDS,
+            )
+            copy.start()
+            sends.append(copy)
+
+    for h in range(PIECES):
+        span = pl.ds(h * piece, piece)
+        for peer in [partner] + others:
+            arrival(out_ref.at[span, columns(peer)], rg.at[h, peer], peer).wait_recv()
+    for copy in sends:
+        copy.wait_send()
+
+
+def exchange(part, aux, backward):
+    n = lax.axis_size("tensor")
+    rows, width = part.shape
+    cols = width // n
+    vmem = pl.BlockSpec(memory_space=pltpu.VMEM)
+    gathered = jax.ShapeDtypeStruct((rows, width), jnp.bfloat16)
+    own = jax.ShapeDtypeStruct((rows, cols), jnp.float32)
+    dma = pltpu.SemaphoreType.DMA
+    return pl.pallas_call(
+        functools.partial(exchange_kernel, n, backward),
+        out_shape=gathered if backward else (gathered, own),
+        in_specs=[vmem, vmem],
+        out_specs=vmem if backward else (vmem, vmem),
+        scratch_shapes=[
+            pltpu.VMEM((rows, cols), jnp.float32),
+            pltpu.VMEM((rows, cols), jnp.float32),
+            pltpu.VMEM((n - 2, rows, cols), jnp.bfloat16),
+            pltpu.VMEM((n, rows, cols), jnp.bfloat16),
+            dma((PIECES,)),
+            dma((PIECES,)),
+            dma((PIECES, n - 2)),
+            dma((PIECES, n)),
+            dma((PIECES, n - 1)),
+            dma((PIECES, n)),
+        ],
+        compiler_params=pltpu.CompilerParams(
+            collective_id=1 if backward else 0,
+            has_side_effects=True,
+            vmem_limit_bytes=32 * 1024 * 1024,
+        ),
+        cost_estimate=pl.CostEstimate(
+            flops=20 * rows * cols, bytes_accessed=rows * width * 6, transcendentals=rows * cols
+        ),
+    )(part, aux)
 
 
 def slot_table(routes, group_count, capacity):
@@ -97,27 +262,11 @@
         precision=lax.Precision.HIGH,
         preferred_element_type=jnp.float32,
     )
-    lat_size = pre_part.shape[1]
-    lat_cols = lat_size // tensor_size
-
-    def scatter_latents(part):
-        blocks = part.reshape(rows, tensor_size, lat_cols).transpose(1, 0, 2)
-        own = lax.psum_scatter(blocks, "tensor", scatter_dimension=0, tiled=True)
-        return own.reshape(rows, lat_cols)
-
-    def gather_latents(own):
-        blocks = lax.all_gather(own.astype(jnp.bfloat16), "tensor", axis=0, tiled=False)
-        return blocks.transpose(1, 0, 2).reshape(rows, lat_size)
-
-    bias_own = lax.dynamic_slice_in_dim(
-        enc_bias[0], lax.axis_index("tensor") * lat_cols, lat_cols
-    )
-    pre_own = scatter_latents(pre_part) + bias_own[None, :]
-    latent_own, gelu_back = jax.vjp(activation, pre_own)
-    latent = gather_latents(latent_own)
+    latent, pre_own = exchange(pre_part, enc_bias, False)
     partial_out = jnp.dot(
-        latent,
-        dec_weight[0].astype(jnp.bfloat16),
+        latent.astype(jnp.float32),
+        dec_weight[0],
+        precision=lax.Precision.HIGH,
         preferred_element_type=jnp.float32,
     )
     back_parts = lax.all_to_all(
@@ -151,14 +300,13 @@
         precision=lax.Precision.HIGH,
         preferred_element_type=jnp.float32,
     )
-    latent_sum = scatter_latents(latent_part)
     dec_grad = lax.dot_general(
         latent,
         error_flat.astype(jnp.bfloat16),
         (((0,), (0,)), ((), ())),
         preferred_element_type=jnp.float32,
     )
-    pre_grad = gather_latents(gelu_back(latent_sum)[0])
+    pre_grad = exchange(latent_part, pre_own, True)
     enc_grad = lax.dot_general(
         inputs_flat,
         pre_grad,

time: 330 us -> 345 us (1.045)
  Pallas kernels: 0 us -> 150 us
  waiting for transfers between devices: 150 us -> 26.8 us
  blocking collectives: 42.8 us -> 72.3 us
  local copies, waits for them, and re-layouts: 19.8 us -> 2.49 us
  starting transfers between devices: 15.8 us -> 7.4 us
  matrix products: 76.5 us -> 68.3 us
  other arithmetic: 10.3 us -> 3.45 us
    pallas_call x0 -> x2, Pallas kernels: none -> 150 us  [exchange(): pl.pallas_call(functools.partial(exchange_kernel, n, backward), out_shape...]
    reduce_scatter x2 -> x0, waiting for transfers between devices: 61.2 us -> none  [scatter_latents(): own = lax.psum_scatter(blocks, 'tensor', scatter_dimension=0, tiled=True)]
    all_to_all x0 -> x2, blocking collectives: none -> 38.9 us  [the longest x1 26.9 us: on_device(): lax.all_to_all(jnp.repeat(packed, span_size, axis=0), 'expert', split_axi...]
    all_gather x2 -> x0, waiting for transfers between devices: 30.4 us -> none  [gather_latents(): lax.all_gather(own.astype(jnp.bfloat16), 'tensor', axis=0, tiled=False)]
    all_to_all x2 -> x0, waiting for transfers between devices: 24 us -> none  [the longest x1 24 us: on_device(): lax.all_to_all(jnp.repeat(packed, span_size, axis=0), 'expert', split_axi...]
    dot_general x2 -> x0, local copies, waits for them, and re-layouts: 13.8 us -> none  [the longest x1 12.6 us: on_device(): jnp.dot(inputs_flat.astype(jnp.float32), enc_weight[0], precision=lax.Pre...]
    reduce_scatter x1, waiting for transfers between devices: 10.3 us -> 0.01 us  [on_device(): lax.psum_scatter(mixed, 'tensor', scatter_dimension=0, tiled=True)]
    all_gather x1, blocking collectives: 30.8 us -> 21.5 us  [on_device(): full_tokens = lax.all_gather(tokens, 'tensor', axis=1, tiled=True)]
  transfers between devices with their start and end apart: 9 -> 3, of which waited for: 6 -> 2; matrix products, arithmetic and copies ran while one was open for 19% -> 5% of each run, Pallas kernels for 0% -> 23%
where the time goes in v2:
time: 345 us
  Pallas kernels  150 us (43%)
  blocking collectives  72.3 us (21%)
  matrix products  68.3 us (20%)
  waiting for transfers between devices  26.8 us (8%)
  between operations  14.2 us (4%)
  starting transfers between devices  7.4 us (2%)
  other arithmetic  3.45 us (1%)
    pallas_call x2, Pallas kernels, exchange(): pl.pallas_call(functools.partial(exchange_kernel, n, backward), out_shape...  150 us
    all_to_all x1, blocking collectives, on_device(): lax.all_to_all(jnp.repeat(packed, span_size, axis=0), 'expert', split_axi...  26.9 us
    all_to_all x1, waiting for transfers between devices, on_device(): lax.all_to_all(part_rows, 'expert', split_axis=0, concat_axis=0, tiled=True)  22.6 us
    all_gather x1, blocking collectives, on_device(): full_tokens = lax.all_gather(tokens, 'tensor', axis=1, tiled=True)  21.5 us
    dot_general x1, matrix products, on_device(): jnp.dot(hidden, down_weight[0], preferred_element_type=jnp.float32)  18.7 us
    all_to_all x1, blocking collectives, on_device(): lax.all_to_all(partial_out.reshape(sources, CAP_S, col_width), 'expert',...  12 us
    all_to_all x1, blocking collectives, on_device(): lax.all_to_all(error_slots, 'expert', split_axis=0, concat_axis=0, tiled=...  11.9 us
    dot_general x1, matrix products, on_device(): lax.dot_general(error_flat, dec_weight[0], (((1,), (1,)), ((), ())), prec...  9.24 us
  transfers between devices with their start and end apart: 3, of which 2 were waited for; matrix products, arithmetic and copies ran while one was open for 5% of the time, Pallas kernels for 23%

profile of v2, /device:TPU:0, one launch (start us, length us, event | category | flops | bytes accessed | tf_op | source)
XLA Modules:
  0.0 345.0 jit_solution(10875615125175203139)
XLA Ops:
  7.2 0.8 copy.40
  8.1 0.1 eq.76
  8.2 1.2 reduce-window.6
  9.9 0.1 reduce_sum.51
  10.1 0.7 multiply_add_fusion
  10.8 21.5 %all_gather.3 = bf16[128,3072]{1,0:T(8,128)(2,1)S(1)} all-gather(bf16[128,768]{1,0:T(8,128)(2,1)} %param.10), channel_id=1, replica_groups=mesh['groups'=2,'expert'=4,'tensor'=4] {'tensor'}, dimensions={1}, use_global_device_ids=true | all-gather | bytes 983040 | tf_op jit(solution)/shard_map/all_gather | solution.py:217
  32.3 0.7 convolution_convert_fusion
  33.0 26.9 %all_to_all.25 = bf16[4,80,3072]{2,1,0:T(8,128)(2,1)S(1)} all-to-all(bf16[4,80,3072]{2,1,0:T(8,128)(2,1)S(1)} %bitcast.97), channel_id=1, replica_groups=mesh['groups'=2,'expert'=4,'tensor'=4] {'expert'}, dimensions={0} | all-to-all | bytes 3932160 | tf_op jit(solution)/shard_map/all_to_all | solution.py:222
  59.9 8.8 %fusion.4 = f32[320,2048]{1,0:T(8,128)} fusion(bf16[320,3072]{1,0:T(8,128)(2,1)S(1)} %bitcast.107, bf16[1,3072,2048]{2,1,0:T(8,128)(2,1)} %param.14), kind=kOutput, calls=%fused_computation.4 | convolution fusion | flops 4026531840 | bytes 17170432 | tf_op jit(solution)/shard_map/dot_general | solution.py:227
  68.6 18.7 %fusion.12 = bf16[320,3072]{1,0:T(8,128)(2,1)} fusion(bf16[1,2048,3072]{2,1,0:T(8,128)(2,1)} %param.16, bf16[320,3072]{1,0:T(8,128)(2,1)S(1)} %bitcast.108, bf16[1,3072,2048]{2,1,0:T(8,128)(2,1)} %param.15, f32[320,2048]{1,0:T(8,128)} %fusion.4), kind=kOutput, calls=%fused_computation.15 | convolution fusion | flops 8057978880 | bytes 31719424 | tf_op jit(solution)/shard_map/dot_general | solution.py:230
  87.4 3.7 %all-to-all-start.3 = ((bf16[4,80,3072]{2,1,0:T(8,128)(2,1)}), bf16[4,80,3072]{2,1,0:T(8,128)(2,1)S(1)}, u32[]{:S(2)}, u32[]{:S(2)}) async-start(bf16[4,80,3072]{2,1,0:T(8,128)(2,1)} %bitcast.106), calls=%async_computation.3 | async-start | bytes 3932160 | tf_op jit(solution)/shard_map/all_to_all | solution.py:232
  91.2 0.2 reduce_window_sum.26
  91.4 0.2 select_reduce_fusion.1
  91.7 1.1 convolution_convert_fusion.2
  92.7 22.6 %all-to-all-done.3 = bf16[4,80,3072]{2,1,0:T(8,128)(2,1)S(1)} async-done(((bf16[4,80,3072]{2,1,0:T(8,128)(2,1)}), bf16[4,80,3072]{2,1,0:T(8,128)(2,1)S(1)}, u32[]{:S(2)}, u32[]{:S(2)}) %all-to-all-start.3) | async-done | bytes 1966112 | tf_op jit(solution)/shard_map/all_to_all | solution.py:232
  115.4 3.5 %all-to-all-start = ((bf16[4,48,768]{2,1,0:T(8,128)(2,1)}), bf16[4,48,768]{2,1,0:T(8,128)(2,1)S(1)}, u32[]{:S(2)}, u32[]{:S(2)}) async-start(bf16[4,48,768]{2,1,0:T(8,128)(2,1)} %bitcast.3), calls=%async_computation | async-start | bytes 589824 | tf_op jit(solution)/shard_map/all_to_all | solution.py:255
  118.8 0.2 reduce-scatter.2.cloned.1.call-start
  119.1 1.0 convolution_convert_fusion.1
  120.1 0.9 copy.50
  121.1 4.1 %all-to-all-done = bf16[4,48,768]{2,1,0:T(8,128)(2,1)S(1)} async-done(((bf16[4,48,768]{2,1,0:T(8,128)(2,1)}), bf16[4,48,768]{2,1,0:T(8,128)(2,1)S(1)}, u32[]{:S(2)}, u32[]{:S(2)}) %all-to-all-start) | async-done | bytes 294944 | tf_op jit(solution)/shard_map/all_to_all | solution.py:255
  125.2 6.3 %fusion.10.part_ref = f32[192,4096]{1,0:T(8,128)S(1)} fusion(bf16[192,768]{1,0:T(8,128)(2,1)S(1)} %bitcast.102, f32[1,768,4096]{2,1,0:T(8,128)} %param.17), kind=kOutput, calls=%fused_computation.10 | convolution fusion | flops 3623878656 | bytes 16023552 | tf_op jit(solution)/shard_map/dot_general | solution.py:259
  131.5 78.7 %shard_map.121 = (bf16[192,4096]{1,0:T(8,128)(2,1)S(1)}, f32[192,1024]{1,0:T(8,128)S(1)}) custom-call(f32[192,4096]{1,0:T(8,128)S(1)} %fusion.10.part_ref, f32[1,4096]{1,0:T(1,128)S(1)} %copy-done), custom_call_target="tpu_custom_call" | custom-call | flops 3932160 | bytes 4718592 | tf_op jit(solution)/shard_map/pallas_call | solution.py:156
  210.2 7.4 %fusion.6 = f32[4,48,768]{2,1,0:T(8,128)S(1)} fusion(bf16[4,48,4096]{2,1,0:T(8,128)(2,1)S(1)} %bitcast.95, f32[1,4096,768]{2,1,0:T(8,128)} %param.19), kind=kOutput, calls=%fused_computation.6 | convolution fusion | flops 3623878656 | bytes 14745600 | tf_op jit(solution)/shard_map/dot_general | solution.py:266
  217.7 12.0 %all_to_all.26 = f32[4,48,768]{2,1,0:T(8,128)S(1)} all-to-all(f32[4,48,768]{2,1,0:T(8,128)S(1)} %fusion.6), channel_id=1, replica_groups=mesh['groups'=2,'expert'=4,'tensor'=4] {'expert'}, dimensions={0} | all-to-all | bytes 1179648 | tf_op jit(solution)/shard_map/all_to_all | solution.py:272
  229.7 1.3 fusion.21
  231.0 0.5 fusion.26
  231.5 11.9 %all_to_all.27 = f32[4,48,768]{2,1,0:T(8,128)S(1)} all-to-all(f32[4,48,768]{2,1,0:T(8,128)S(1)} %bitcast.105), channel_id=1, replica_groups=mesh['groups'=2,'expert'=4,'tensor'=4] {'expert'}, dimensions={0} | all-to-all | bytes 1179648 | tf_op jit(solution)/shard_map/all_to_all | solution.py:294
  243.5 9.2 %fusion.8.part_ref = f32[192,4096]{1,0:T(8,128)S(1)} fusion(f32[192,768]{1,0:T(8,128)S(1)} %bitcast.98, f32[1,4096,768]{2,1,0:T(8,128)} %param.19), kind=kOutput, calls=%fused_computation.8 | convolution fusion | flops 3623878656 | bytes 16318464 | tf_op jit(solution)/shard_map/dot_general | solution.py:296
  252.7 6.7 %convolution_bitcast_fusion = f32[1,4096,768]{2,1,0:T(8,128)} fusion(bf16[192,4096]{1,0:T(8,128)(2,1)S(1)} %get-tuple-element.5, f32[192,768]{1,0:T(8,128)S(1)} %bitcast.99), kind=kOutput, calls=%fused_computation.12 | convolution fusion | flops 1208107008 | bytes 14745600 | tf_op jit(solution)/shard_map/dot_general | solution.py:303
  259.4 71.3 %shard_map.122 = bf16[192,4096]{1,0:T(8,128)(2,1)S(1)} custom-call(f32[192,4096]{1,0:T(8,128)S(1)} %fusion.8.part_ref, f32[192,1024]{1,0:T(8,128)S(1)} %get-tuple-element.6.aux_ref), custom_call_target="tpu_custom_call" | custom-call | flops 3932160 | bytes 4718592 | tf_op jit(solution)/shard_map/pallas_call | solution.py:156
  330.6 0.9 convert_reduce_fusion
  331.5 6.6 %convolution_bitcast_fusion.1 = f32[1,768,4096]{2,1,0:T(8,128)} fusion(bf16[192,768]{1,0:T(8,128)(2,1)S(1)} %bitcast.103, bf16[192,4096]{1,0:T(8,128)(2,1)S(1)} %shard_map.122), kind=kOutput, calls=%fused_computation.13 | convolution fusion | flops 1207959552 | bytes 14450688 | tf_op jit(solution)/shard_map/dot_general | solution.py:310
  (26 shorter events, 0.8 us)
Async XLA Ops:
  87.4 3.7 %copy-start.2 = (s32[128,1]{0,1:T(1,128)S(1)}, s32[128,1]{0,1:T(1,128)}, u32[]{:S(2)}) copy-start(s32[128,1]{0,1:T(1,128)} %param.13) | copy-start | bytes 1540
  87.4 4.0 %copy-start.3 = (f32[128]{0:T(128)S(1)}, f32[128]{0:T(128)}, u32[]{:S(2)}) copy-start(f32[128]{0:T(128)} %param.12) | copy-start | bytes 1540
  87.4 4.3 %copy-start.1 = (bf16[128,768]{1,0:T(8,128)(2,1)S(1)}, bf16[128,768]{1,0:T(8,128)(2,1)}, u32[]{:S(2)}) copy-start(bf16[128,768]{1,0:T(8,128)(2,1)} %param.10) | copy-start | bytes 589828
  87.4 28.0 %all-to-all-start.3 = ((bf16[4,80,3072]{2,1,0:T(8,128)(2,1)}), bf16[4,80,3072]{2,1,0:T(8,128)(2,1)S(1)}, u32[]{:S(2)}, u32[]{:S(2)}) async-start(bf16[4,80,3072]{2,1,0:T(8,128)(2,1)} %bitcast.106), calls=%async_computation.3 | async-start | bytes 3932160 | tf_op jit(solution)/shard_map/all_to_all | solution.py:232
  115.4 9.8 %all-to-all-start = ((bf16[4,48,768]{2,1,0:T(8,128)(2,1)}), bf16[4,48,768]{2,1,0:T(8,128)(2,1)S(1)}, u32[]{:S(2)}, u32[]{:S(2)}) async-start(bf16[4,48,768]{2,1,0:T(8,128)(2,1)} %bitcast.3), calls=%async_computation | async-start | bytes 589824 | tf_op jit(solution)/shard_map/all_to_all | solution.py:255
  118.8 110.9 %reduce-scatter.2.cloned.1.call-start = ((), (), s32[]{:S(2)}) async-start(), calls=%async_computation.6 | async-start | bytes 983040 | tf_op jit(solution)/shard_map/reduce_scatter | solution.py:243
  125.2 6.3 %copy-start = (f32[1,4096]{1,0:T(1,128)S(1)}, f32[1,4096]{1,0:T(1,128)}, u32[]{:S(2)}) copy-start(f32[1,4096]{1,0:T(1,128)} %aux_ref.1) | copy-start | bytes 49156
Sparse Core Ops, SparseCore 0:
  122.6 31.4 reduce-scatter.1

commit v3 on v2

--- a/solution.py
+++ b/solution.py
@@ -262,7 +262,22 @@
         precision=lax.Precision.HIGH,
         preferred_element_type=jnp.float32,
     )
-    latent, pre_own = exchange(pre_part, enc_bias, False)
+    lat_size = pre_part.shape[1]
+    lat_cols = lat_size // tensor_size
+    blocks = lax.optimization_barrier(pre_part).reshape(rows, tensor_size, lat_cols)
+    pre_own = lax.psum_scatter(
+        blocks.transpose(1, 0, 2), "tensor", scatter_dimension=0, tiled=True
+    ).reshape(rows, lat_cols)
+    bias_own = lax.dynamic_slice_in_dim(
+        enc_bias[0], lax.axis_index("tensor") * lat_cols, lat_cols
+    )
+    pre_own = pre_own + bias_own[None, :]
+    latent_own = 0.5 * pre_own * (1.0 + gelu_tail(pre_own))
+    latent = (
+        lax.all_gather(latent_own.astype(jnp.bfloat16), "tensor", axis=0, tiled=False)
+        .transpose(1, 0, 2)
+        .reshape(rows, lat_size)
+    )
     partial_out = jnp.dot(
         latent.astype(jnp.float32),
         dec_weight[0],

time: 345 us -> 295 us (0.86)
  Pallas kernels: 150 us -> 70.9 us
  waiting for transfers between devices: 26.8 us -> 65.1 us
  blocking collectives: 72.3 us -> 40.5 us
  starting transfers between devices: 7.4 us -> 15.2 us
  local copies, waits for them, and re-layouts: 2.49 us -> 9.96 us
  other arithmetic: 3.45 us -> 6.98 us
    pallas_call x2 -> x1, Pallas kernels: 150 us -> 70.9 us  [exchange(): pl.pallas_call(functools.partial(exchange_kernel, n, backward), out_shape...]
    all_to_all x3 -> x1, blocking collectives: 50.8 us -> 10.4 us  [on_device(): lax.all_to_all(outgoing, 'expert', split_axis=0, concat_axis=0, tiled=True)]
    all_to_all x1 -> x3, waiting for transfers between devices: 4.13 us -> 32.6 us  [the longest x1 24 us: on_device(): lax.all_to_all(jnp.repeat(packed, span_size, axis=0), 'expert', split_axi...]
    all_gather x1, blocking collectives: 21.5 us -> 30.1 us  [on_device(): full_tokens = lax.all_gather(tokens, 'tensor', axis=1, tiled=True)]
    reduce_scatter x1, waiting for transfers between devices: 0.01 us -> 8.53 us  [on_device(): lax.psum_scatter(mixed, 'tensor', scatter_dimension=0, tiled=True)]
    all_to_all x1 -> x3, starting transfers between devices: 3.45 us -> 10.9 us  [the longest x1 3.74 us: on_device(): lax.all_to_all(error_slots, 'expert', split_axis=0, concat_axis=0, tiled=...]
    reshape x0 -> x2, local copies, waits for them, and re-layouts: none -> 3.65 us  [the longest x1 2.08 us: on_device(): lax.optimization_barrier(pre_part).reshape(rows, tensor_size, lat_cols)]
  transfers between devices with their start and end apart: 3 -> 7, of which waited for: 2 -> 5; matrix products, arithmetic and copies ran while one was open for 5% -> 16% of each run, Pallas kernels for 23% -> 0%
where the time goes in v3:
time: 295 us; the launch traced here: 294 us
  matrix products  71.6 us (24%)
  Pallas kernels  70.9 us (24%)
  waiting for transfers between devices  65.1 us (22%)
  blocking collectives  40.5 us (14%)
  starting transfers between devices  15.2 us (5%)
  between operations  14 us (5%)
  local copies, waits for them, and re-layouts  9.96 us (3%)
  other arithmetic  6.98 us (2%)
    pallas_call x1, Pallas kernels, exchange(): pl.pallas_call(functools.partial(exchange_kernel, n, backward), out_shape...  70.9 us
    all_gather x1, blocking collectives, on_device(): full_tokens = lax.all_gather(tokens, 'tensor', axis=1, tiled=True)  30.1 us
    all_to_all x1, waiting for transfers between devices, on_device(): lax.all_to_all(jnp.repeat(packed, span_size, axis=0), 'expert', split_axi...  24 us
    all_to_all x1, waiting for transfers between devices, on_device(): lax.all_to_all(part_rows, 'expert', split_axis=0, concat_axis=0, tiled=True)  23.9 us
    dot_general x1, matrix products, on_device(): jnp.dot(hidden, down_weight[0], preferred_element_type=jnp.float32)  19 us
    all_to_all x1, blocking collectives, on_device(): lax.all_to_all(outgoing, 'expert', split_axis=0, concat_axis=0, tiled=True)  10.4 us
    dot_general x1, matrix products, on_device(): lax.dot_general(error_flat, dec_weight[0], (((1,), (1,)), ((), ())), prec...  9.24 us
    dot_general x1, matrix products, on_device(): jnp.dot(flat_rows, gate_weight[0], preferred_element_type=jnp.float32)  8.77 us
  transfers between devices with their start and end apart: 7, of which 5 were waited for; matrix products, arithmetic and copies ran while one was open for 16% of the time, Pallas kernels for 0%

profile of v3, /device:TPU:0, one launch (start us, length us, event | category | flops | bytes accessed | tf_op | source)
XLA Modules:
  0.0 294.3 jit_solution(6337078890705820079)
XLA Ops:
  9.6 1.3 convolution_convert_fusion.2
  10.9 10.4 %all_to_all.25 = bf16[4,48,768]{2,1,0:T(8,128)(2,1)S(1)} all-to-all(bf16[4,48,768]{2,1,0:T(8,128)(2,1)S(1)} %bitcast.124), channel_id=1, replica_groups=mesh['groups'=2,'expert'=4,'tensor'=4] {'expert'}, dimensions={0} | all-to-all | bytes 589824 | tf_op jit(solution)/shard_map/all_to_all | solution.py:255
  21.3 6.2 %fusion.10 = f32[192,4096]{1,0:T(8,128)S(1)} fusion(bf16[192,768]{1,0:T(8,128)(2,1)S(1)} %bitcast.118, f32[1,768,4096]{2,1,0:T(8,128)} %param.17), kind=kOutput, calls=%fused_computation.10 | convolution fusion | flops 3623878656 | bytes 16023552 | tf_op jit(solution)/shard_map/dot_general | solution.py:259
  27.5 2.1 copy.65
  30.7 1.2 reduce-window.6
  32.6 30.1 %all_gather.8 = bf16[128,3072]{1,0:T(8,128)(2,1)S(1)} all-gather(bf16[128,768]{1,0:T(8,128)(2,1)S(1)} %copy-done.3), channel_id=1, replica_groups=mesh['groups'=2,'expert'=4,'tensor'=4] {'tensor'}, dimensions={1}, use_global_device_ids=true | all-gather | bytes 983040 | tf_op jit(solution)/shard_map/all_gather | solution.py:217
  62.7 1.9 convolution_convert_fusion
  64.7 3.6 %all-to-all-start.2 = ((bf16[4,80,3072]{2,1,0:T(8,128)(2,1)}), bf16[4,80,3072]{2,1,0:T(8,128)(2,1)S(1)}, u32[]{:S(2)}, u32[]{:S(2)}) async-start(bf16[4,80,3072]{2,1,0:T(8,128)(2,1)} %bitcast.16), calls=%async_computation.3 | async-start | bytes 3932160 | tf_op jit(solution)/shard_map/all_to_all | solution.py:222
  68.5 24.0 %all-to-all-done.2 = bf16[4,80,3072]{2,1,0:T(8,128)(2,1)S(1)} async-done(((bf16[4,80,3072]{2,1,0:T(8,128)(2,1)}), bf16[4,80,3072]{2,1,0:T(8,128)(2,1)S(1)}, u32[]{:S(2)}, u32[]{:S(2)}) %all-to-all-start.2) | async-done | bytes 1966112 | tf_op jit(solution)/shard_map/all_to_all | solution.py:222
  92.5 8.8 %fusion.4 = f32[320,2048]{1,0:T(8,128)} fusion(bf16[320,3072]{1,0:T(8,128)(2,1)S(1)} %bitcast.121, bf16[1,3072,2048]{2,1,0:T(8,128)(2,1)} %param.14), kind=kOutput, calls=%fused_computation.4 | convolution fusion | flops 4026531840 | bytes 17170432 | tf_op jit(solution)/shard_map/dot_general | solution.py:227
  101.3 2.1 fusion.28
  103.5 19.0 %fusion.12 = bf16[320,3072]{1,0:T(8,128)(2,1)} fusion(bf16[1,2048,3072]{2,1,0:T(8,128)(2,1)} %param.16, bf16[320,3072]{1,0:T(8,128)(2,1)S(1)} %bitcast.122, bf16[1,3072,2048]{2,1,0:T(8,128)(2,1)} %param.15, f32[320,2048]{1,0:T(8,128)} %fusion.4), kind=kOutput, calls=%fused_computation.15 | convolution fusion | flops 8057978880 | bytes 31719424 | tf_op jit(solution)/shard_map/dot_general | solution.py:230
  122.5 3.7 %all-to-all-start.3 = ((bf16[4,80,3072]{2,1,0:T(8,128)(2,1)}), bf16[4,80,3072]{2,1,0:T(8,128)(2,1)S(1)}, u32[]{:S(2)}, u32[]{:S(2)}) async-start(bf16[4,80,3072]{2,1,0:T(8,128)(2,1)} %bitcast.123), calls=%async_computation.4 | async-start | bytes 3932160 | tf_op jit(solution)/shard_map/all_to_all | solution.py:232
  126.5 23.9 %all-to-all-done.3 = bf16[4,80,3072]{2,1,0:T(8,128)(2,1)S(1)} async-done(((bf16[4,80,3072]{2,1,0:T(8,128)(2,1)}), bf16[4,80,3072]{2,1,0:T(8,128)(2,1)S(1)}, u32[]{:S(2)}, u32[]{:S(2)}) %all-to-all-start.3) | async-done | bytes 1966112 | tf_op jit(solution)/shard_map/all_to_all | solution.py:232
  150.5 1.0 convolution_convert_fusion.1
  151.5 0.9 copy.66
  152.5 2.6 copy.50
  155.1 1.2 dot_general.43
  156.3 8.4 %fusion.6 = f32[4,48,768]{2,1,0:T(8,128)} fusion(bf16[4,48,4096]{2,1,0:T(8,128)(2,1)S(1)} %dot_general.43, f32[1,4096,768]{2,1,0:T(8,128)} %param.19), kind=kOutput, calls=%fused_computation.6 | convolution fusion | flops 3623878656 | bytes 14745600 | tf_op jit(solution)/shard_map/dot_general | solution.py:281
  164.7 3.6 %all-to-all-start.1 = ((f32[4,48,768]{2,1,0:T(8,128)}), f32[4,48,768]{2,1,0:T(8,128)S(1)}, u32[]{:S(2)}, u32[]{:S(2)}) async-start(f32[4,48,768]{2,1,0:T(8,128)} %fusion.6), calls=%async_computation.2 | async-start | bytes 1179648 | tf_op jit(solution)/shard_map/all_to_all | solution.py:287
  168.3 8.5 %reduce-scatter.5.cloned.1.call-done = bf16[1,128,768]{2,1,0:T(8,128)(2,1)} async-done(((bf16[4,128,768]{2,1,0:T(8,128)(2,1)}), bf16[1,128,768]{2,1,0:T(8,128)(2,1)}) %reduce-scatter.5.cloned.1.call-update) | async-done | bytes 196624 | tf_op jit(solution)/shard_map/reduce_scatter | solution.py:243
  176.8 1.0 all-to-all-done.1
  177.8 1.3 fusion.21
  179.2 1.3 fusion.32
  180.5 3.7 %all-to-all-start.4 = ((f32[4,48,768]{2,1,0:T(8,128)}), f32[4,48,768]{2,1,0:T(8,128)S(1)}, u32[]{:S(2)}, u32[]{:S(2)}) async-start(f32[4,48,768]{2,1,0:T(8,128)} %bitcast.25), calls=%async_computation.6 | async-start | bytes 1179648 | tf_op jit(solution)/shard_map/all_to_all | solution.py:309
  184.3 1.6 copy.60
  185.9 7.6 %all-to-all-done.4 = f32[4,48,768]{2,1,0:T(8,128)S(1)} async-done(((f32[4,48,768]{2,1,0:T(8,128)}), f32[4,48,768]{2,1,0:T(8,128)S(1)}, u32[]{:S(2)}, u32[]{:S(2)}) %all-to-all-start.4) | async-done | bytes 589856 | tf_op jit(solution)/shard_map/all_to_all | solution.py:309
  193.5 9.2 %fusion.8.part_ref = f32[192,4096]{1,0:T(8,128)S(1)} fusion(f32[192,768]{1,0:T(8,128)S(1)} %bitcast.115, f32[1,4096,768]{2,1,0:T(8,128)} %param.19), kind=kOutput, calls=%fused_computation.8 | convolution fusion | flops 3623878656 | bytes 16318464 | tf_op jit(solution)/shard_map/dot_general | solution.py:311
  202.7 70.9 %shard_map.121 = bf16[192,4096]{1,0:T(8,128)(2,1)S(1)} custom-call(f32[192,4096]{1,0:T(8,128)S(1)} %fusion.8.part_ref, f32[192,1024]{1,0:T(8,128)S(1)} %bitcast_add_fusion.aux_ref), custom_call_target="tpu_custom_call" | custom-call | flops 3932160 | bytes 4718592 | tf_op jit(solution)/shard_map/pallas_call | solution.py:156
  273.6 0.9 convert_reduce_fusion
  274.5 6.6 %convolution_bitcast_fusion.1 = f32[1,768,4096]{2,1,0:T(8,128)} fusion(bf16[192,768]{1,0:T(8,128)(2,1)S(1)} %bitcast.119, bf16[192,4096]{1,0:T(8,128)(2,1)S(1)} %shard_map.121), kind=kOutput, calls=%fused_computation.13 | convolution fusion | flops 1207959552 | bytes 14450688 | tf_op jit(solution)/shard_map/dot_general | solution.py:325
  281.2 6.7 %convolution_bitcast_fusion = f32[1,4096,768]{2,1,0:T(8,128)} fusion(bf16[192,4096]{1,0:T(8,128)(2,1)S(1)} %bitcast.112, bf16[192,768]{1,0:T(8,128)(2,1)S(1)} %bitcast.125), kind=kOutput, calls=%fused_computation.12 | convolution fusion | flops 1207959552 | bytes 14450688 | tf_op jit(solution)/shard_map/dot_general | solution.py:318
  (45 shorter events, 4.9 us)
Async XLA Ops:
  7.2 61.3 %copy-start = (f32[1,4096]{1,0:T(1,128)S(1)}, f32[1,4096]{1,0:T(1,128)}, u32[]{:S(2)}) copy-start(f32[1,4096]{1,0:T(1,128)} %param.18) | copy-start | bytes 49156
  7.2 94.1 %reduce-scatter.3.cloned.1.call-start = ((), (), s32[]{:S(2)}) async-start(), calls=%async_computation.7 | async-start | bytes 3932160 | tf_op jit(solution)/shard_map/reduce_scatter | solution.py:268
  29.6 0.7 copy-start.4
  29.6 3.0 %copy-start.3 = (bf16[128,768]{1,0:T(8,128)(2,1)S(1)}, bf16[128,768]{1,0:T(8,128)(2,1)}, u32[]{:S(2)}) copy-start(bf16[128,768]{1,0:T(8,128)(2,1)} %param.10) | copy-start | bytes 589828
  64.7 27.9 %all-to-all-start.2 = ((bf16[4,80,3072]{2,1,0:T(8,128)(2,1)}), bf16[4,80,3072]{2,1,0:T(8,128)(2,1)S(1)}, u32[]{:S(2)}, u32[]{:S(2)}) async-start(bf16[4,80,3072]{2,1,0:T(8,128)(2,1)} %bitcast.16), calls=%async_computation.3 | async-start | bytes 3932160 | tf_op jit(solution)/shard_map/all_to_all | solution.py:222
  68.3 84.2 %all-gather.2.cloned.1.call-start = ((), (), s32[]{:S(2)}) async-start(), calls=%async_computation.8 | async-start | bytes 1966080 | tf_op jit(solution)/shard_map/all_gather | solution.py:277
  122.5 4.0 %copy-start.5 = (f32[128]{0:T(128)S(1)}, f32[128]{0:T(128)}, u32[]{:S(2)}) copy-start(f32[128]{0:T(128)} %param.12) | copy-start | bytes 1540
  122.5 28.0 %all-to-all-start.3 = ((bf16[4,80,3072]{2,1,0:T(8,128)(2,1)}), bf16[4,80,3072]{2,1,0:T(8,128)(2,1)S(1)}, u32[]{:S(2)}, u32[]{:S(2)}) async-start(bf16[4,80,3072]{2,1,0:T(8,128)(2,1)} %bitcast.123), calls=%async_computation.4 | async-start | bytes 3932160 | tf_op jit(solution)/shard_map/all_to_all | solution.py:232
  126.2 50.7 %reduce-scatter.5.cloned.1.call-start = ((), (), s32[]{:S(2)}) async-start(), calls=%async_computation.9 | async-start | bytes 983040 | tf_op jit(solution)/shard_map/reduce_scatter | solution.py:243
  164.7 19.5 %copy-start.2 = (f32[1,192,1024]{2,1,0:T(8,128)S(1)}, f32[1,192,1024]{2,1,0:T(8,128)}, u32[]{:S(2)}) copy-start(f32[1,192,1024]{2,1,0:T(8,128)} %reduce-scatter.3.cloned.1.call-done) | copy-start | bytes 2359300
  164.7 13.1 %all-to-all-start.1 = ((f32[4,48,768]{2,1,0:T(8,128)}), f32[4,48,768]{2,1,0:T(8,128)S(1)}, u32[]{:S(2)}, u32[]{:S(2)}) async-start(f32[4,48,768]{2,1,0:T(8,128)} %fusion.6), calls=%async_computation.2 | async-start | bytes 1179648 | tf_op jit(solution)/shard_map/all_to_all | solution.py:287
  180.5 13.0 %all-to-all-start.4 = ((f32[4,48,768]{2,1,0:T(8,128)}), f32[4,48,768]{2,1,0:T(8,128)S(1)}, u32[]{:S(2)}, u32[]{:S(2)}) async-start(f32[4,48,768]{2,1,0:T(8,128)} %bitcast.25), calls=%async_computation.6 | async-start | bytes 1179648 | tf_op jit(solution)/shard_map/all_to_all | solution.py:309
  281.1 6.7 %copy-start.1 = (f32[1,4096]{1,0:T(1,128)S(1)}, f32[1,4096]{1,0:T(1,128)}, u32[]{:S(2)}) copy-start(f32[1,4096]{1,0:T(1,128)} %param.18) | copy-start | bytes 49156
Sparse Core Ops, SparseCore 0:
  29.7 71.5 reduce-scatter.2
  103.6 38.1 all-gather.1
  152.6 24.2 reduce-scatter.4
